TPU v7x, 256 devices: a whole 4x4x8 slice. The times are simulated.
256 devices in a mesh: section: 16 (over x_hi, z), dp: 16 (over x_lo, y, core).
Axes of the slice: x: 4 (x_hi: 2, x_lo: 2; x = x_hi * 2 + x_lo), y: 4, z: 8, core: 2. Of those that a mesh axis runs over, the one named last changes fastest.
Arguments:
- stash: bfloat16 [16, 2048, 8192], P('section', 'dp'), may hold values from -6 to 6
- query: bfloat16 [16, 2048, 4096], P('section', 'dp')
- grad_out: bfloat16 [16, 2048, 4096], P('section', 'dp'), may hold values from -6 to 6
- kv_weight: bfloat16 [16, 8192, 1024], P('section', 'dp'), may hold values from -0.0625 to 0.0625
- doc_ids: int32 [16, 2048], P('section', 'dp'), may hold values from 0 to 63, never falling along the last dimension, each value on 1 to 128 neighbouring positions
- evicted: int32 [16], replicated, may hold values from 0 to 1, as said below
Outputs:
- next_grad: bfloat16 [16, 2048, 8192], P('section', 'dp')
- weight_grad: bfloat16 [16, 8192, 1024], P('section', 'dp')
- query_grad: bfloat16 [16, 2048, 4096], P('section', 'dp')
Inputs may be any that keep to these rules, and one draw needn't show every extreme that they name: evicted[i] equals evicted[15 - i]; both values occur in every draw. `doc_ids`: never falls along a row.
All inputs are finite; a program needn't handle non-finite values.
Results may differ from a plain program's by a relative error of at most 0.025.
The roundings to bfloat16 on the way count: a program that leaves them out, or rounds other values in their place, can miss the bound.
Values may be sent and summed in bfloat16 or wider, within the bound.
A program may use at most 128 MiB of HBM per device.

v0:
```python
import jax
import jax.numpy as jnp
from jax import lax
from jax.sharding import PartitionSpec as P

QHEADS = 32
KVHEADS = 4
HEAD_DIM = 128


def swapped(block, axis, stride):
    count = lax.axis_size(axis)
    route = []
    for low in range(count):
        high = low | 1 << stride
        if high != low and high < count:
            route += [(low, high), (high, low)]
    return lax.ppermute(block, axis, route)


def shifted(array, axis, by):
    count = lax.axis_size(axis)
    pairs = [(i, i + by) for i in range(count) if 0 <= i + by < count]
    return lax.ppermute(array, axis, pairs)


def attend_back(queries, upstream, keyvalue, seg_ids):
    tok_count = queries.shape[0]
    group = QHEADS // KVHEADS
    width = KVHEADS * HEAD_DIM
    scale = HEAD_DIM ** (-0.5)
    q_heads = queries.reshape(tok_count, KVHEADS, group, HEAD_DIM)
    d_heads = upstream.reshape(tok_count, KVHEADS, group, HEAD_DIM)
    keys = keyvalue[:, :width].reshape(tok_count, KVHEADS, HEAD_DIM)
    values = keyvalue[:, width:].reshape(tok_count, KVHEADS, HEAD_DIM)
    scores = jnp.einsum("ihgd,jhd->hgij", q_heads, keys, preferred_element_type=jnp.float32) * scale
    rows_pos = jnp.arange(tok_count)[:, None]
    cols_pos = jnp.arange(tok_count)[None, :]
    allowed = (seg_ids[:, None] == seg_ids[None, :]) & (cols_pos <= rows_pos)
    scores = jnp.where(allowed, scores, -1e30)
    peak = jnp.max(scores, axis=-1, keepdims=True)
    raised = jnp.exp(scores - peak)
    probs = raised / jnp.sum(raised, axis=-1, keepdims=True)
    probs_low = probs.astype(jnp.bfloat16)
    output = jnp.einsum("hgij,jhd->ihgd", probs_low, values, preferred_element_type=jnp.float32)
    delta = jnp.einsum("ihgd,ihgd->hgi", d_heads.astype(jnp.float32), output)
    grad_values = jnp.einsum(
        "hgij,ihgd->jhd", probs_low, d_heads, preferred_element_type=jnp.float32
    )
    grad_probs = jnp.einsum("ihgd,jhd->hgij", d_heads, values, preferred_element_type=jnp.float32)
    grad_scores = (probs * (grad_probs - delta[..., None])).astype(jnp.bfloat16)
    grad_keys = (
        jnp.einsum("hgij,ihgd->jhd", grad_scores, q_heads, preferred_element_type=jnp.float32)
        * scale
    )
    grad_query = (
        jnp.einsum("hgij,jhd->ihgd", grad_scores, keys, preferred_element_type=jnp.float32) * scale
    )
    grad_kv = jnp.concatenate(
        [grad_keys.reshape(tok_count, width), grad_values.reshape(tok_count, width)], axis=1
    )
    return (
        grad_kv.astype(jnp.bfloat16),
        grad_query.reshape(tok_count, QHEADS * HEAD_DIM).astype(jnp.bfloat16),
    )


def local(stash, query, grad_out, kv_weight, doc_ids, evicted):
    held_slot = stash[0]
    queries = query[0]
    upstream = grad_out[0]
    weight_shard = kv_weight[0]
    seg_ids = doc_ids[0]
    sections = lax.axis_size("section")
    levels = sections.bit_length() - 1
    fetched = held_slot
    for bit_number in range(levels):
        fetched = swapped(fetched, "section", bit_number)
    position = lax.axis_index("section")
    layer_input = jnp.where(evicted[position] == 1, fetched, held_slot)
    replicas = lax.axis_size("dp")
    x_columns = lax.all_to_all(layer_input, "dp", split_axis=1, concat_axis=0, tiled=True)
    x_part = x_columns
    keyvalue = lax.psum_scatter(
        jnp.dot(x_part, weight_shard, preferred_element_type=jnp.float32),
        "dp",
        scatter_dimension=0,
        tiled=True,
    ).astype(jnp.bfloat16)
    grad_kv, grad_query = attend_back(queries, upstream, keyvalue, seg_ids)
    portion = lax.all_gather(grad_kv, "dp", axis=0, tiled=True)
    x_part = x_columns
    grad_sum = jnp.einsum("tc,tk->ck", x_part, portion, preferred_element_type=jnp.float32)
    rows_grad = jnp.einsum("tk,ck->tc", portion, weight_shard, preferred_element_type=jnp.float32)
    input_cols = rows_grad.astype(jnp.bfloat16)
    weight_total, input_cols = (grad_sum, input_cols)
    input_grad = lax.all_to_all(input_cols, "dp", split_axis=0, concat_axis=1, tiled=True)
    weight_out = (weight_total / replicas).astype(jnp.bfloat16)
    passed = shifted(input_grad, "section", -1)
    return (passed[None], weight_out[None], grad_query[None])


def solution(mesh):
    placed = (
        P("section", "dp", None),
        P("section", "dp", None),
        P("section", "dp", None),
        P("section", "dp", None),
        P("section", "dp"),
        P(),
    )
    return jax.shard_map(
        local,
        mesh=mesh,
        in_specs=placed,
        out_specs=(P("section", "dp", None), P("section", "dp", None), P("section", "dp", None)),
        check_vma=False,
    )
```

profile of v0, /device:TPU:249, one launch (start us, length us, event | category | flops | bytes accessed | tf_op | source)
XLA Modules:
  0.0 575.3 jit_solution(521112396826199081)
XLA Ops:
  7.2 3.3 copy.33
  11.4 45.8 %collective-permute-done = bf16[128,8192]{0,1:T(8,128)(2,1)S(1)} collective-permute-done((bf16[128,8192]{0,1:T(8,128)(2,1)S(1)}, bf16[128,8192]{0,1:T(8,128)(2,1)S(1)}, u32[]{:S(2)}, u32[]{:S(2)}) %collective-permute-start) | collective-permute-done | bytes 2097184 | tf_op jit(solution)/shard_map/ppermute | solution.py:18
  58.3 91.7 %collective-permute-done.1 = bf16[128,8192]{0,1:T(8,128)(2,1)S(1)} collective-permute-done((bf16[128,8192]{0,1:T(8,128)(2,1)S(1)}, bf16[128,8192]{0,1:T(8,128)(2,1)S(1)}, u32[]{:S(2)}, u32[]{:S(2)}) %collective-permute-start.1) | collective-permute-done | bytes 2097184 | tf_op jit(solution)/shard_map/ppermute | solution.py:18
  150.0 1.6 collective-permute-start.2
  151.6 93.5 %collective-permute-done.2 = bf16[128,8192]{0,1:T(8,128)(2,1)} collective-permute-done((bf16[128,8192]{0,1:T(8,128)(2,1)S(1)}, bf16[128,8192]{0,1:T(8,128)(2,1)}, u32[]{:S(2)}, u32[]{:S(2)}) %collective-permute-start.2) | collective-permute-done | bytes 2097184 | tf_op jit(solution)/shard_map/ppermute | solution.py:18
  245.1 2.7 collective-permute-start.3
  249.1 44.5 %collective-permute-done.3 = bf16[128,8192]{0,1:T(8,128)(2,1)} collective-permute-done((bf16[128,8192]{0,1:T(8,128)(2,1)}, bf16[128,8192]{0,1:T(8,128)(2,1)}, u32[]{:S(2)}, u32[]{:S(2)}) %collective-permute-start.3) | collective-permute-done | bytes 2097184 | tf_op jit(solution)/shard_map/ppermute | solution.py:18
  293.8 32.2 %all_to_all.38 = bf16[128,16,512]{0,2,1:T(8,128)(2,1)S(1)} all-to-all(bf16[128,16,512]{0,2,1:T(8,128)(2,1)S(1)} %bitcast.85), channel_id=1, replica_groups=mesh['section'=16,'dp'=16] {'dp'}, dimensions={1} | all-to-all | bytes 4194304 | tf_op jit(solution)/shard_map/all_to_all | solution.py:82
  325.9 2.6 copy.34
  328.5 7.2 %fusion.9 = f32[2048,1024]{1,0:T(8,128)} fusion(bf16[2048,512]{1,0:T(8,128)(2,1)} %bitcast.91, bf16[1,512,1024]{2,1,0:T(8,128)(2,1)S(1)} %copy-done), kind=kOutput, calls=%fused_computation.20 | convolution fusion | flops 2147483648 | bytes 11534336 | tf_op jit(solution)/shard_map/dot_general | solution.py:85
  339.0 1.7 copy.44
  340.8 69.8 %reduce-scatter.2.cloned.1.call-done = f32[128,1024]{1,0:T(8,128)} async-done(((f32[2048,1024]{1,0:T(8,128)}), f32[128,1024]{1,0:T(8,128)}) %reduce-scatter.2.cloned.1.call-update) | async-done | bytes 524304 | tf_op jit(solution)/shard_map/reduce_scatter | solution.py:84
  412.1 2.2 fusion.23
  414.3 3.3 convolution_bitcast_fusion
  417.7 3.1 copy.58
  420.8 2.3 multiply_reduce_fusion
  423.2 2.5 fusion.7
  427.9 47.6 %all-gather.2.cloned.1.call-done = bf16[2048,1024]{0,1:T(8,128)(2,1)} async-done(((bf16[128,1024]{0,1:T(8,128)(2,1)}), bf16[2048,1024]{0,1:T(8,128)(2,1)}) %all-gather.2.cloned.1.call-update) | async-done | bytes 4194320 | tf_op jit(solution)/shard_map/all_gather | solution.py:91
  475.5 4.6 convolution_convert_fusion
  480.1 30.9 %all_to_all.39 = bf16[16,128,512]{2,1,0:T(8,128)(2,1)S(1)} all-to-all(bf16[16,128,512]{2,1,0:T(8,128)(2,1)S(1)} %bitcast.93), channel_id=1, replica_groups=mesh['section'=16,'dp'=16] {'dp'}, dimensions={0} | all-to-all | bytes 4194304 | tf_op jit(solution)/shard_map/all_to_all | solution.py:97
  512.6 3.0 collective-permute-start.4
  517.3 6.2 %fusion.4 = bf16[1,512,1024]{2,1,0:T(8,128)(2,1)} fusion(bf16[2048,512]{1,0:T(8,128)(2,1)} %bitcast.92, bf16[2048,1024]{0,1:T(8,128)(2,1)} %all-gather.2.cloned.1.call-done), kind=kOutput, calls=%fused_computation.13 | convolution fusion | flops 2148532224 | bytes 7340032 | tf_op jit(solution)/shard_map/tc,tk->ck/dot_general | solution.py:93
  523.5 41.9 %collective-permute-done.4 = bf16[128,8192]{1,0:T(8,128)(2,1)} collective-permute-done((bf16[128,8192]{1,0:T(8,128)(2,1)}, bf16[128,8192]{1,0:T(8,128)(2,1)}, u32[]{:S(2)}, u32[]{:S(2)}) %collective-permute-start.4) | collective-permute-done | bytes 2097184 | tf_op jit(solution)/shard_map/ppermute | solution.py:24
  565.4 3.1 copy.78
  (44 shorter events, 13.2 us)
Async XLA Ops:
  7.2 321.4 %copy-start = (bf16[1,512,1024]{2,1,0:T(8,128)(2,1)S(1)}, bf16[1,512,1024]{2,1,0:T(8,128)(2,1)}, u32[]{:S(2)}) copy-start(bf16[1,512,1024]{2,1,0:T(8,128)(2,1)} %param.9) | copy-start | bytes 3145732
  7.2 240.6 %copy-start.6 = (s32[16]{0:T(128)S(1)}, s32[16]{0:T(128)}, u32[]{:S(2)}) copy-start(s32[16]{0:T(128)} %param.11) | copy-start | bytes 196
  7.2 403.5 %reduce-scatter.2.cloned.1.call-start = ((), (), s32[]{:S(2)}) async-start(), calls=%async_computation.3 | async-start | bytes 8912896 | tf_op jit(solution)/shard_map/reduce_scatter | solution.py:84
  10.5 46.6 %collective-permute-start = (bf16[128,8192]{0,1:T(8,128)(2,1)S(1)}, bf16[128,8192]{0,1:T(8,128)(2,1)S(1)}, u32[]{:S(2)}, u32[]{:S(2)}) collective-permute-start(bf16[128,8192]{0,1:T(8,128)(2,1)S(1)} %bitcast.84), channel_id=1, source_target_pairs={{0,16},{16,0},{32,48},{48,32},{64,80},{80,64},{96,112},{112,96},{1... | collective-permute-start | bytes 6291464 | tf_op jit(solution)/shard_map/ppermute | solution.py:18
  57.1 92.9 %collective-permute-start.1 = (bf16[128,8192]{0,1:T(8,128)(2,1)S(1)}, bf16[128,8192]{0,1:T(8,128)(2,1)S(1)}, u32[]{:S(2)}, u32[]{:S(2)}) collective-permute-start(bf16[128,8192]{0,1:T(8,128)(2,1)S(1)} %collective-permute-done), channel_id=1, source_target_pairs={{0,32},{32,0},{16,48},{48,16},{64,96},{96,64},{80,112},{112,80},{1... | collective-permute-start | bytes 6291464 | tf_op jit(solution)/shard_map/ppermute | solution.py:18
  150.0 95.1 %collective-permute-start.2 = (bf16[128,8192]{0,1:T(8,128)(2,1)S(1)}, bf16[128,8192]{0,1:T(8,128)(2,1)}, u32[]{:S(2)}, u32[]{:S(2)}) collective-permute-start(bf16[128,8192]{0,1:T(8,128)(2,1)S(1)} %collective-permute-done.1), channel_id=1, source_target_pairs={{0,64},{64,0},{16,80},{80,16},{32,96},{96,32},{48,112},{112,48},{1... | collective-permute-start | bytes 6291464 | tf_op jit(solution)/shard_map/ppermute | solution.py:18
  245.1 48.4 %collective-permute-start.3 = (bf16[128,8192]{0,1:T(8,128)(2,1)}, bf16[128,8192]{0,1:T(8,128)(2,1)}, u32[]{:S(2)}, u32[]{:S(2)}) collective-permute-start(bf16[128,8192]{0,1:T(8,128)(2,1)} %collective-permute-done.2), channel_id=1, source_target_pairs={{0,128},{128,0},{16,144},{144,16},{32,160},{160,32},{48,176},{176,... | collective-permute-start | bytes 6291464 | tf_op jit(solution)/shard_map/ppermute | solution.py:18
  335.7 1.2 copy-start.1
  335.7 139.8 %all-gather.2.cloned.1.call-start = ((), (), s32[]{:S(2)}) async-start(), calls=%async_computation.4 | async-start | bytes 4456448 | tf_op jit(solution)/shard_map/all_gather | solution.py:91
  337.6 3.2 copy-start.5
  412.1 2.2 copy-start.3
  414.3 3.4 copy-start.8
  423.2 2.5 copy-start.2
  423.2 2.5 copy-start.4
  423.2 2.9 copy-start.7
  423.2 2.9 copy-start.9
  512.6 52.8 %collective-permute-start.4 = (bf16[128,8192]{1,0:T(8,128)(2,1)}, bf16[128,8192]{1,0:T(8,128)(2,1)}, u32[]{:S(2)}, u32[]{:S(2)}) collective-permute-start(bf16[128,8192]{1,0:T(8,128)(2,1)} %bitcast.36), channel_id=1, source_target_pairs={{16,0},{32,16},{48,32},{64,48},{80,64},{96,80},{112,96},{128,112},... | collective-permute-start | bytes 6291464 | tf_op jit(solution)/shard_map/ppermute | solution.py:24
Sparse Core Ops, SparseCore 0:
  335.8 74.7 reduce-scatter.1
  428.0 47.4 all-gather.1
where the time goes:
time: 577 us; the launch traced here: 575 us
  waiting for transfers between devices  435 us (75%)
  blocking collectives  63.1 us (11%)
  matrix products  27.3 us (5%)
  local copies, waits for them, and re-layouts  21.2 us (4%)
  between operations  14.9 us (3%)
  starting transfers between devices  9.58 us (2%)
    ppermute x4, waiting for transfers between devices, swapped(): return lax.ppermute(block, axis, route)  275 us
    reduce_scatter x1, waiting for transfers between devices, local(): lax.psum_scatter(jnp.dot(x_part, weight_shard, preferred_element_type=jnp...  69.8 us
    all_gather x1, waiting for transfers between devices, local(): portion = lax.all_gather(grad_kv, 'dp', axis=0, tiled=True)  47.6 us
    ppermute x1, waiting for transfers between devices, shifted(): return lax.ppermute(array, axis, pairs)  41.9 us
    all_to_all x1, blocking collectives, local(): lax.all_to_all(layer_input, 'dp', split_axis=1, concat_axis=0, tiled=True)  32.2 us
    all_to_all x1, blocking collectives, local(): lax.all_to_all(input_cols, 'dp', split_axis=0, concat_axis=1, tiled=True)  30.9 us
    unnamed x25, local copies, waits for them, and re-layouts  13.7 us
  transfers between devices with their start and end apart: 7, of which 7 were waited for; matrix products, arithmetic and copies ran while one was open for 2% of the time, Pallas kernels for 0%

commit v1 on v0

--- a/solution.py
+++ b/solution.py
@@ -8,14 +8,9 @@
 HEAD_DIM = 128
 
 
-def swapped(block, axis, stride):
+def mirrored(block, axis):
     count = lax.axis_size(axis)
-    route = []
-    for low in range(count):
-        high = low | 1 << stride
-        if high != low and high < count:
-            route += [(low, high), (high, low)]
-    return lax.ppermute(block, axis, route)
+    return lax.ppermute(block, axis, [(i, count - 1 - i) for i in range(count)])
 
 
 def shifted(array, axis, by):
@@ -71,11 +66,7 @@
     upstream = grad_out[0]
     weight_shard = kv_weight[0]
     seg_ids = doc_ids[0]
-    sections = lax.axis_size("section")
-    levels = sections.bit_length() - 1
-    fetched = held_slot
-    for bit_number in range(levels):
-        fetched = swapped(fetched, "section", bit_number)
+    fetched = mirrored(held_slot, "section")
     position = lax.axis_index("section")
     layer_input = jnp.where(evicted[position] == 1, fetched, held_slot)
     replicas = lax.axis_size("dp")

time: 577 us -> 391 us (0.68)
  waiting for transfers between devices: 435 us -> 254 us
  starting transfers between devices: 9.58 us -> 3.34 us
    ppermute x4 -> x1, waiting for transfers between devices: 275 us -> 93.9 us  [mirrored(): return lax.ppermute(block, axis, [(i, count - 1 - i) for i in range(count)])]
    ppermute x4 -> x1, starting transfers between devices: 6.33 us -> 0.09 us  [mirrored(): return lax.ppermute(block, axis, [(i, count - 1 - i) for i in range(count)])]
  transfers between devices with their start and end apart: 7 -> 4, of which waited for: 7 -> 4; matrix products, arithmetic and copies ran while one was open for 2% -> 3% of each run, Pallas kernels for 0% -> 0%
where the time goes in v1:
time: 391 us; the launch traced here: 389 us
  waiting for transfers between devices  254 us (65%)
  blocking collectives  63.2 us (16%)
  matrix products  27.3 us (7%)
  local copies, waits for them, and re-layouts  21.4 us (5%)
  between operations  14.9 us (4%)
  other arithmetic  4.38 us (1%)
    ppermute x1, waiting for transfers between devices, mirrored(): return lax.ppermute(block, axis, [(i, count - 1 - i) for i in range(count)])  93.9 us
    reduce_scatter x1, waiting for transfers between devices, local(): lax.psum_scatter(jnp.dot(x_part, weight_shard, preferred_element_type=jnp...  71.1 us
    all_gather x1, waiting for transfers between devices, local(): portion = lax.all_gather(grad_kv, 'dp', axis=0, tiled=True)  47.6 us
    ppermute x1, waiting for transfers between devices, shifted(): return lax.ppermute(array, axis, pairs)  41.7 us
    all_to_all x1, blocking collectives, local(): lax.all_to_all(layer_input, 'dp', split_axis=1, concat_axis=0, tiled=True)  32.3 us
    all_to_all x1, blocking collectives, local(): lax.all_to_all(input_cols, 'dp', split_axis=0, concat_axis=1, tiled=True)  30.9 us
    unnamed x25, local copies, waits for them, and re-layouts  13.9 us
  transfers between devices with their start and end apart: 4, of which 4 were waited for; matrix products, arithmetic and copies ran while one was open for 3% of the time, Pallas kernels for 0%

profile of v1, /device:TPU:249, one launch (start us, length us, event | category | flops | bytes accessed | tf_op | source)
XLA Modules:
  0.0 389.0 jit_solution(7079359879356836009)
XLA Ops:
  7.2 3.3 copy.33
  11.9 93.9 %collective-permute-done = bf16[128,8192]{0,1:T(8,128)(2,1)} collective-permute-done((bf16[128,8192]{0,1:T(8,128)(2,1)S(1)}, bf16[128,8192]{0,1:T(8,128)(2,1)}, u32[]{:S(2)}, u32[]{:S(2)}) %collective-permute-start) | collective-permute-done | bytes 2097184 | tf_op jit(solution)/shard_map/ppermute | solution.py:13
  106.0 32.3 %all_to_all.38 = bf16[128,16,512]{0,2,1:T(8,128)(2,1)S(1)} all-to-all(bf16[128,16,512]{0,2,1:T(8,128)(2,1)S(1)} %bitcast.85), channel_id=1, replica_groups=mesh['section'=16,'dp'=16] {'dp'}, dimensions={1} | all-to-all | bytes 4194304 | tf_op jit(solution)/shard_map/all_to_all | solution.py:73
  138.3 2.6 copy.34
  140.9 7.2 %fusion.9 = f32[2048,1024]{1,0:T(8,128)} fusion(bf16[2048,512]{1,0:T(8,128)(2,1)} %bitcast.91, bf16[1,512,1024]{2,1,0:T(8,128)(2,1)S(1)} %copy-done), kind=kOutput, calls=%fused_computation.20 | convolution fusion | flops 2147483648 | bytes 11534336 | tf_op jit(solution)/shard_map/dot_general | solution.py:76
  148.2 1.1 copy-done.1
  150.0 1.4 copy.76
  151.4 1.7 copy.44
  153.2 71.1 %reduce-scatter.2.cloned.1.call-done = f32[128,1024]{1,0:T(8,128)} async-done(((f32[2048,1024]{1,0:T(8,128)}), f32[128,1024]{1,0:T(8,128)}) %reduce-scatter.2.cloned.1.call-update) | async-done | bytes 524304 | tf_op jit(solution)/shard_map/reduce_scatter | solution.py:75
  224.3 1.1 convert_element_type.33
  225.8 2.2 fusion.23
  228.0 3.3 convolution_bitcast_fusion
  231.3 3.2 copy.58
  234.5 2.3 multiply_reduce_fusion
  236.9 2.5 fusion.7
  241.6 47.6 %all-gather.2.cloned.1.call-done = bf16[2048,1024]{0,1:T(8,128)(2,1)} async-done(((bf16[128,1024]{0,1:T(8,128)(2,1)}), bf16[2048,1024]{0,1:T(8,128)(2,1)}) %all-gather.2.cloned.1.call-update) | async-done | bytes 4194320 | tf_op jit(solution)/shard_map/all_gather | solution.py:82
  289.2 4.6 %convolution_convert_fusion = bf16[2048,512]{1,0:T(8,128)(2,1)S(1)} fusion(bf16[2048,1024]{0,1:T(8,128)(2,1)} %all-gather.2.cloned.1.call-done, bf16[1,512,1024]{2,1,0:T(8,128)(2,1)S(1)} %copy-done), kind=kOutput, calls=%fused_computation.1 | convolution fusion | flops 2148532224 | bytes 7340032 | tf_op jit(solution)/shard_map/tk,ck->tc/dot_general | solution.py:85
  293.8 30.9 %all_to_all.39 = bf16[16,128,512]{2,1,0:T(8,128)(2,1)S(1)} all-to-all(bf16[16,128,512]{2,1,0:T(8,128)(2,1)S(1)} %bitcast.93), channel_id=1, replica_groups=mesh['section'=16,'dp'=16] {'dp'}, dimensions={0} | all-to-all | bytes 4194304 | tf_op jit(solution)/shard_map/all_to_all | solution.py:88
  324.7 1.6 copy.75
  326.3 3.2 collective-permute-start.1
  329.9 1.3 copy.48
  331.2 6.2 %fusion.4 = bf16[1,512,1024]{2,1,0:T(8,128)(2,1)} fusion(bf16[2048,512]{1,0:T(8,128)(2,1)} %bitcast.92, bf16[2048,1024]{0,1:T(8,128)(2,1)} %all-gather.2.cloned.1.call-done), kind=kOutput, calls=%fused_computation.13 | convolution fusion | flops 2148532224 | bytes 7340032 | tf_op jit(solution)/shard_map/tc,tk->ck/dot_general | solution.py:84
  337.4 41.7 %collective-permute-done.1 = bf16[128,8192]{1,0:T(8,128)(2,1)} collective-permute-done((bf16[128,8192]{1,0:T(8,128)(2,1)}, bf16[128,8192]{1,0:T(8,128)(2,1)}, u32[]{:S(2)}, u32[]{:S(2)}) %collective-permute-start.1) | collective-permute-done | bytes 2097184 | tf_op jit(solution)/shard_map/ppermute | solution.py:19
  379.1 3.1 copy.78
  (38 shorter events, 4.8 us)
Async XLA Ops:
  7.2 133.8 %copy-start = (bf16[1,512,1024]{2,1,0:T(8,128)(2,1)S(1)}, bf16[1,512,1024]{2,1,0:T(8,128)(2,1)}, u32[]{:S(2)}) copy-start(bf16[1,512,1024]{2,1,0:T(8,128)(2,1)} %param.9) | copy-start | bytes 3145732
  7.2 3.5 copy-start.6
  7.2 217.2 %reduce-scatter.2.cloned.1.call-start = ((), (), s32[]{:S(2)}) async-start(), calls=%async_computation.3 | async-start | bytes 8912896 | tf_op jit(solution)/shard_map/reduce_scatter | solution.py:75
  10.5 95.2 %collective-permute-start = (bf16[128,8192]{0,1:T(8,128)(2,1)S(1)}, bf16[128,8192]{0,1:T(8,128)(2,1)}, u32[]{:S(2)}, u32[]{:S(2)}) collective-permute-start(bf16[128,8192]{0,1:T(8,128)(2,1)S(1)} %bitcast.84), channel_id=1, source_target_pairs={{0,240},{16,224},{32,208},{48,192},{64,176},{80,160},{96,144},{112... | collective-permute-start | bytes 6291464 | tf_op jit(solution)/shard_map/ppermute | solution.py:13
  148.1 1.2 copy-start.1
  148.1 141.1 %all-gather.2.cloned.1.call-start = ((), (), s32[]{:S(2)}) async-start(), calls=%async_computation.4 | async-start | bytes 4456448 | tf_op jit(solution)/shard_map/all_gather | solution.py:82
  150.0 3.2 copy-start.5
  225.8 2.2 copy-start.3
  228.0 3.3 copy-start.8
  236.9 2.5 copy-start.2
  236.9 2.5 copy-start.4
  236.9 2.9 copy-start.7
  236.9 2.9 copy-start.9
  326.3 52.8 %collective-permute-start.1 = (bf16[128,8192]{1,0:T(8,128)(2,1)}, bf16[128,8192]{1,0:T(8,128)(2,1)}, u32[]{:S(2)}, u32[]{:S(2)}) collective-permute-start(bf16[128,8192]{1,0:T(8,128)(2,1)} %bitcast.36), channel_id=1, source_target_pairs={{16,0},{32,16},{48,32},{64,48},{80,64},{96,80},{112,96},{128,112},... | collective-permute-start | bytes 6291464 | tf_op jit(solution)/shard_map/ppermute | solution.py:19
Sparse Core Ops, SparseCore 0:
  148.2 76.0 reduce-scatter.1
  241.7 47.4 all-gather.1

commit v2 on v1

v2 whole, which is shorter than its diff:
```python
import jax
import jax.numpy as jnp
from jax import lax
from jax.experimental import pallas as pl
from jax.experimental.pallas import tpu as pltpu
from jax.sharding import PartitionSpec as P

QHEADS = 32
KVHEADS = 4
HEAD_DIM = 128
GROUP = QHEADS // KVHEADS
WIDTH = KVHEADS * HEAD_DIM
MESH = pl.DeviceIdType.MESH
MIB = 1024 * 1024
N_DP = 16
N_SENDS = 30


def remote(src, dst, send_sem, recv_sem, target):
    return pltpu.make_async_remote_copy(
        src_ref=src,
        dst_ref=dst,
        send_sem=send_sem,
        recv_sem=recv_sem,
        device_id=target,
        device_id_type=MESH,
    )


class Gather:
    def __init__(self, own_half, buf, send_sem, recv_sem):
        self.own_half, self.buf = own_half, buf
        self.send_sem, self.recv_sem = send_sem, recv_sem
        self.sent = []
        me = lax.axis_index("dp")
        x, y, core = me // 8, (me % 8) // 2, me % 2
        at = lambda far, step, other: (
            (1 - x if far else x) * 8
            + lax.rem(y + step, 4) * 2
            + (1 - core if other else core)
        )
        self.at = at
        self.me = me
        self.up, self.down = at(0, 1, 0), at(0, 3, 0)
        self.across, self.sibling = at(1, 0, 0), at(0, 0, 1)

    def slot(self, far, step, half, other=0):
        return self.at(far, step, other) * 2 + half

    def send(self, slot, target, src=None):
        where = self.buf.at[slot]
        copy = remote(
            where if src is None else src,
            where,
            self.send_sem.at[len(self.sent)],
            self.recv_sem.at[slot],
            {"dp": target},
        )
        copy.start()
        self.sent.append(copy)

    def wait(self, slot):
        where = self.buf.at[slot]
        remote(where, where, self.send_sem.at[0], self.recv_sem.at[slot], {"dp": self.up}).wait_recv()

    def start(self):
        for half in range(2):
            slot, src = self.slot(0, 0, half), self.own_half(half)
            for target in (self.across, self.up, self.down, self.sibling):
                self.send(slot, target, src)

    def forward(self, far, step, half, targets):
        slot = self.slot(far, step, half)
        self.wait(slot)
        for target in targets:
            self.send(slot, target)

    def relay(self):
        up, down, sibling = self.up, self.down, self.sibling
        self.forward(0, 3, 0, (up, sibling))
        self.forward(0, 1, 0, (sibling,))
        self.forward(1, 0, 0, (up, down, sibling))
        self.forward(0, 1, 1, (down, sibling))
        self.forward(0, 3, 1, (sibling,))
        self.forward(1, 0, 1, (up, down, sibling))
        self.forward(0, 2, 0, (sibling,))
        self.forward(0, 2, 1, (sibling,))
        self.forward(1, 3, 0, (up, sibling))
        self.forward(1, 1, 0, (sibling,))
        self.forward(1, 1, 1, (down, sibling))
        self.forward(1, 3, 1, (sibling,))
        self.forward(1, 2, 0, (sibling,))
        self.forward(1, 2, 1, (sibling,))

    def finish(self):
        for far in range(2):
            for step in range(4):
                for half in range(2):
                    self.wait(self.slot(far, step, half, 1))

    def drain(self):
        for copy in self.sent:
            copy.wait_send()


def greet(targets):
    barrier = pltpu.get_barrier_semaphore()
    for target in targets:
        pl.semaphore_signal(barrier, inc=1, device_id=target, device_id_type=MESH)
    pl.semaphore_wait(barrier, len(targets))


def columns(index, width):
    return pl.ds(pl.multiple_of(index * width, width), width)


def pre_kernel(
    stash_ref, weight_ref, evicted_ref, x_ref, whole_ref, kv_ref,
    wbuf, fetched, held, xbuf, total,
    w_send, w_recv, m_send, m_recv, local_sem,
):
    section = lax.axis_index("section")
    mirror = {"section": 15 - section}
    depth = weight_ref.shape[0]
    half_rows = depth // 2
    gather = Gather(lambda half: weight_ref.at[pl.ds(half * half_rows, half_rows)], wbuf, w_send, w_recv)
    me = gather.me
    greet([mirror] + [{"dp": t} for t in (gather.up, gather.down, gather.across, gather.sibling)])
    gather.start()

    def mirrored(chunk):
        at = columns(chunk, depth)
        return remote(stash_ref.at[:, at], fetched.at[:, at], m_send.at[chunk], m_recv.at[chunk], mirror)

    for chunk in range(N_DP):
        mirrored(chunk).start()
    own_copies = [
        pltpu.make_async_copy(weight_ref.at[pl.ds(h * half_rows, half_rows)], wbuf.at[2 * me + h], local_sem.at[h])
        for h in range(2)
    ]
    held_copy = pltpu.make_async_copy(stash_ref, held, local_sem.at[2])
    for copy in own_copies:
        copy.start()
    held_copy.start()
    for copy in own_copies:
        copy.wait()
    held_copy.wait()
    gather.relay()
    gather.finish()
    whole_copy = pltpu.make_async_copy(wbuf, whole_ref, local_sem.at[3])
    whole_copy.start()

    total[...] = jnp.zeros_like(total)
    moved = evicted_ref[section] == 1

    @pl.loop(0, N_DP)
    def _(chunk):
        at = columns(chunk, depth)
        mirrored(chunk).wait_recv()
        part = jnp.where(moved, fetched[:, at], held[:, at])
        xbuf[:, at] = part
        for half in range(2):
            total[...] += jnp.dot(
                part[:, half * half_rows:(half + 1) * half_rows],
                wbuf[2 * chunk + half],
                preferred_element_type=jnp.float32,
            )

    x_copy = pltpu.make_async_copy(xbuf, x_ref, local_sem.at[4])
    x_copy.start()
    kv_ref[...] = total[...].astype(kv_ref.dtype)

    @pl.loop(0, N_DP)
    def _(chunk):
        mirrored(chunk).wait_send()

    gather.drain()
    x_copy.wait()
    whole_copy.wait()


def pre(stash, weight, evicted):
    tok, features = stash.shape
    depth, width = weight.shape
    bf16 = jnp.bfloat16
    any_space = pl.BlockSpec(memory_space=pl.ANY)
    return pl.pallas_call(
        pre_kernel,
        out_shape=(
            jax.ShapeDtypeStruct((tok, features), bf16),
            jax.ShapeDtypeStruct((2 * N_DP, depth // 2, width), bf16),
            jax.ShapeDtypeStruct((tok, width), bf16),
        ),
        in_specs=[any_space, any_space, pl.BlockSpec(memory_space=pltpu.SMEM)],
        out_specs=(any_space, any_space, pl.BlockSpec(memory_space=pltpu.VMEM)),
        scratch_shapes=[
            pltpu.VMEM((2 * N_DP, depth // 2, width), bf16),
            pltpu.VMEM((tok, features), bf16),
            pltpu.VMEM((tok, features), bf16),
            pltpu.VMEM((tok, features), bf16),
            pltpu.VMEM((tok, width), jnp.float32),
            pltpu.SemaphoreType.DMA((N_SENDS,)),
            pltpu.SemaphoreType.DMA((2 * N_DP,)),
            pltpu.SemaphoreType.DMA((N_DP,)),
            pltpu.SemaphoreType.DMA((N_DP,)),
            pltpu.SemaphoreType.DMA((5,)),
        ],
        compiler_params=pltpu.CompilerParams(
            collective_id=0, has_side_effects=True, vmem_limit_bytes=48 * MIB
        ),
        name="pre",
    )(stash, weight, evicted)


def attend_kernel(q_ref, d_ref, kv_ref, col_ref, row_ref, dq_ref, g_ref):
    head = pl.program_id(0)
    tok = q_ref.shape[0]
    scale = HEAD_DIM ** -0.5
    at_k = columns(head, HEAD_DIM)
    at_v = pl.ds(pl.multiple_of(WIDTH + head * HEAD_DIM, HEAD_DIM), HEAD_DIM)
    keys, values = kv_ref[:, at_k], kv_ref[:, at_v]
    stack = lambda ref: jnp.concatenate(
        [ref[:, h * HEAD_DIM:(h + 1) * HEAD_DIM] for h in range(GROUP)], axis=0
    )
    f32 = jnp.float32
    nt = lambda a, b: lax.dot_general(a, b, (((1,), (1,)), ((), ())), preferred_element_type=f32)
    tn = lambda a, b: lax.dot_general(a, b, (((0,), (0,)), ((), ())), preferred_element_type=f32)
    queries, upstream = stack(q_ref), stack(d_ref)
    rows = lax.broadcasted_iota(jnp.int32, (tok, tok), 0)
    cols = lax.broadcasted_iota(jnp.int32, (tok, tok), 1)
    allowed = (col_ref[...] == row_ref[...]) & (cols <= rows)
    scores = (nt(queries, keys) * scale).reshape(GROUP, tok, tok)
    scores = jnp.where(allowed[None], scores, -1e30).reshape(GROUP * tok, tok)
    raised = jnp.exp(scores - jnp.max(scores, axis=-1, keepdims=True))
    probs = raised / jnp.sum(raised, axis=-1, keepdims=True)
    probs_low = probs.astype(jnp.bfloat16)
    output = jnp.dot(probs_low, values, preferred_element_type=f32)
    delta = jnp.sum(upstream.astype(f32) * output, axis=-1, keepdims=True)
    grad_scores = (probs * (nt(upstream, values) - delta)).astype(jnp.bfloat16)
    g_ref[:, at_k] = (tn(grad_scores, queries) * scale).astype(g_ref.dtype)
    g_ref[:, at_v] = tn(probs_low, upstream).astype(g_ref.dtype)
    dq = jnp.dot(grad_scores, keys, preferred_element_type=f32) * scale
    for h in range(GROUP):
        dq_ref[:, h * HEAD_DIM:(h + 1) * HEAD_DIM] = dq[h * tok:(h + 1) * tok].astype(dq_ref.dtype)


def attend(queries, upstream, keyvalue, seg_ids):
    tok = queries.shape[0]
    wide = pl.BlockSpec((tok, GROUP * HEAD_DIM), lambda h: (0, h))
    whole = lambda *shape: pl.BlockSpec(shape, lambda h: (0, 0))
    return pl.pallas_call(
        attend_kernel,
        grid=(KVHEADS,),
        out_shape=(
            jax.ShapeDtypeStruct(queries.shape, jnp.bfloat16),
            jax.ShapeDtypeStruct(keyvalue.shape, jnp.bfloat16),
        ),
        in_specs=[wide, wide, whole(*keyvalue.shape), whole(tok, 1), whole(1, tok)],
        out_specs=(wide, whole(*keyvalue.shape)),
        compiler_params=pltpu.CompilerParams(
            dimension_semantics=("arbitrary",), vmem_limit_bytes=48 * MIB
        ),
        name="attend",
    )(queries, upstream, keyvalue, seg_ids.reshape(tok, 1), seg_ids.reshape(1, tok))


def post_kernel(
    x_ref, whole_ref, g_ref, passed_ref, wgrad_ref,
    wbuf, gbuf, xcols, rows,
    g_send, g_recv, x_send, x_recv, s_send, s_recv, load_sem, local_sem,
):
    section = lax.axis_index("section")
    tok, width = g_ref.shape
    half_rows = wbuf.shape[1]
    depth = 2 * half_rows
    below = {"section": lax.rem(section + 15, 16)}
    above = {"section": lax.rem(section + 1, 16)}
    half_tok = tok // 2
    gather = Gather(lambda half: g_ref.at[pl.ds(half * half_tok, half_tok)], gbuf, g_send, g_recv)
    me = gather.me
    others = [{"dp": lax.rem(me + k, N_DP)} for k in range(1, N_DP)]

    def load(chunk):
        at = pl.ds(2 * chunk, 2)
        return pltpu.make_async_copy(whole_ref.at[at], wbuf.at[at], load_sem.at[chunk])

    for chunk in range(N_DP):
        load(chunk).start()
    own_copies = [
        pltpu.make_async_copy(g_ref.at[pl.ds(h * half_tok, half_tok)], gbuf.at[2 * me + h], local_sem.at[h])
        for h in range(2)
    ]
    own_x = pltpu.make_async_copy(x_ref.at[:, columns(me, depth)], xcols.at[me], local_sem.at[2])
    for copy in own_copies + [own_x]:
        copy.start()
    greet([below, above] + others)
    gather.start()

    def shifted(chunk):
        at = columns(chunk, depth)
        return remote(rows.at[:, at], passed_ref.at[:, at], s_send.at[chunk], s_recv.at[chunk], below)

    @pl.loop(0, N_DP)
    def _(chunk):
        load(chunk).wait()
        for half in range(2):
            at = pl.ds(pl.multiple_of(chunk * depth + half * half_rows, half_rows), half_rows)
            rows[:, at] = lax.dot_general(
                g_ref[...], wbuf[2 * chunk + half], (((1,), (1,)), ((), ())),
                preferred_element_type=jnp.float32,
            ).astype(rows.dtype)
        shifted(chunk).start()

    exchanged = []
    for k, other in zip(range(1, N_DP), others):
        copy = remote(
            x_ref.at[:, columns(other["dp"], depth)], xcols.at[me], x_send.at[k], x_recv.at[k], other
        )
        copy.start()
        exchanged.append(copy)
    gather.relay()
    gather.finish()
    for copy in own_copies + [own_x]:
        copy.wait()
    for k in range(1, N_DP):
        source = lax.rem(me + N_DP - k, N_DP)
        remote(
            xcols.at[source], xcols.at[source], x_send.at[k], x_recv.at[k], {"dp": source}
        ).wait_recv()

    whole_x = xcols[...].reshape(N_DP * tok, depth)
    whole_g = gbuf[...].reshape(N_DP * tok, width)
    for half in range(2):
        at = slice(half * half_rows, (half + 1) * half_rows)
        summed = lax.dot_general(
            whole_x[:, at], whole_g, (((0,), (0,)), ((), ())), preferred_element_type=jnp.float32
        )
        wgrad_ref[at, :] = (summed * (1.0 / N_DP)).astype(wgrad_ref.dtype)

    for copy in exchanged:
        copy.wait_send()
    gather.drain()

    @pl.loop(0, N_DP)
    def _(chunk):
        shifted(chunk).wait()


def post(x, whole, grad_kv):
    tok, features = x.shape
    blocks, half_rows, width = whole.shape
    bf16 = jnp.bfloat16
    any_space = pl.BlockSpec(memory_space=pl.ANY)
    vmem = pl.BlockSpec(memory_space=pltpu.VMEM)
    dma = pltpu.SemaphoreType.DMA
    return pl.pallas_call(
        post_kernel,
        out_shape=(
            jax.ShapeDtypeStruct((tok, features), bf16),
            jax.ShapeDtypeStruct((2 * half_rows, width), bf16),
        ),
        in_specs=[any_space, any_space, vmem],
        out_specs=(any_space, vmem),
        scratch_shapes=[
            pltpu.VMEM((blocks, half_rows, width), bf16),
            pltpu.VMEM((blocks, tok // 2, width), bf16),
            pltpu.VMEM((N_DP, tok, 2 * half_rows), bf16),
            pltpu.VMEM((tok, features), bf16),
            dma((N_SENDS,)), dma((blocks,)),
            dma((N_DP,)), dma((N_DP,)),
            dma((N_DP,)), dma((N_DP,)),
            dma((N_DP,)), dma((3,)),
        ],
        compiler_params=pltpu.CompilerParams(
            collective_id=1, has_side_effects=True, vmem_limit_bytes=48 * MIB
        ),
        name="post",
    )(x, whole, grad_kv)


def local(stash, query, grad_out, kv_weight, doc_ids, evicted):
    x, whole, keyvalue = pre(stash[0], kv_weight[0], evicted)
    grad_query, grad_kv = attend(query[0], grad_out[0], keyvalue, doc_ids[0])
    passed, weight_out = post(x, whole, grad_kv)
    last = lax.axis_index("section") == lax.axis_size("section") - 1
    passed = jnp.where(last, jnp.zeros_like(passed), passed)
    return (passed[None], weight_out[None], grad_query[None])


def solution(mesh):
    rows = P("section", "dp", None)
    return jax.shard_map(
        local,
        mesh=mesh,
        in_specs=(rows, rows, rows, rows, P("section", "dp"), P()),
        out_specs=(rows, rows, rows),
        check_vma=False,
    )
```

time: 391 us -> 220 us (0.56)
  waiting for transfers between devices: 254 us -> 0 us
  Pallas kernels: 0 us -> 208 us
  blocking collectives: 63.2 us -> 0 us
  matrix products: 27.3 us -> 0 us
  local copies, waits for them, and re-layouts: 21.4 us -> 7.09 us
  between operations: 14.9 us -> 0.69 us
    pallas_call x0 -> x3, Pallas kernels: none -> 208 us  [the longest x1 106 us: post(): pl.pallas_call(post_kernel, out_shape=(jax.ShapeDtypeStruct((tok, feature...]
    ppermute x2 -> x0, waiting for transfers between devices: 136 us -> none  [the longest x1 93.9 us: mirrored(): return lax.ppermute(block, axis, [(i, count - 1 - i) for i in range(count)])]
    reduce_scatter x1 -> x0, waiting for transfers between devices: 71.1 us -> none  [local(): lax.psum_scatter(jnp.dot(x_part, weight_shard, preferred_element_type=jnp...]
    all_to_all x2 -> x0, blocking collectives: 63.2 us -> none  [the longest x1 32.3 us: local(): lax.all_to_all(layer_input, 'dp', split_axis=1, concat_axis=0, tiled=True)]
    all_gather x1 -> x0, waiting for transfers between devices: 47.6 us -> none  [local(): portion = lax.all_gather(grad_kv, 'dp', axis=0, tiled=True)]
    dot_general x8 -> x0, matrix products: 25.1 us -> none  [the longest x1 7.17 us: local(): jnp.dot(x_part, weight_shard, preferred_element_type=jnp.float32)]
    unnamed x25 -> x15, local copies, waits for them, and re-layouts: 13.9 us -> 6.98 us
    all_to_all x2 -> x0, local copies, waits for them, and re-layouts: 4.13 us -> none  [the longest x1 2.58 us: local(): lax.all_to_all(layer_input, 'dp', split_axis=1, concat_axis=0, tiled=True)]
  transfers between devices with their start and end apart: 4 -> 0, of which waited for: 4 -> 0; matrix products, arithmetic and copies ran while one was open for 3% -> 0% of each run, Pallas kernels for 0% -> 0%
where the time goes in v2:
time: 220 us; the launch traced here: 219 us
  Pallas kernels  208 us (95%)
  local copies, waits for them, and re-layouts  7.09 us (3%)
  other arithmetic  3.05 us (1%)
    pallas_call x1, Pallas kernels, post(): pl.pallas_call(post_kernel, out_shape=(jax.ShapeDtypeStruct((tok, feature...  106 us
    pallas_call x1, Pallas kernels, pre(): pl.pallas_call(pre_kernel, out_shape=(jax.ShapeDtypeStruct((tok, features...  97.1 us
    unnamed x15, local copies, waits for them, and re-layouts  6.98 us
    pallas_call x1, Pallas kernels, attend(): pl.pallas_call(attend_kernel, grid=(KVHEADS,), out_shape=(jax.ShapeDtypeS...  5.7 us

profile of v2, /device:TPU:249, one launch (start us, length us, event | category | flops | bytes accessed | tf_op | source)
XLA Modules:
  0.0 219.3 jit_solution(9787305763479466508)
XLA Ops:
  0.6 0.0 copy-start.5
  0.6 0.0 copy-start
  0.7 1.6 copy-done
  2.2 0.0 copy-start.2
  2.2 1.2 copy-done.2
  3.5 0.0 copy-start.6
  3.5 0.7 copy-done.6
  4.1 0.0 copy-start.3
  4.1 97.1 %pre.1 = (bf16[128,8192]{1,0:T(8,128)(2,1)S(1)}, bf16[32,256,1024]{2,1,0:T(8,128)(2,1)}, bf16[128,1024]{1,0:T(8,128)(2,1)S(1)}) custom-call(bf16[128,8192]{1,0:T(8,128)(2,1)S(1)} %bitcast.9, bf16[512,1024]{1,0:T(8,128)(2,1)S(1)} %bitcast.10, s32[16]{0:T(128)S(1)} %copy-done.6), custom_call_target="tpu_custom_call" | custom-call | tf_op jit(solution)/shard_map/pre/pallas_call | solution.py:187
  101.3 0.0 copy-done.5
  101.3 0.1 copy.9.col_ref
  101.4 0.0 copy-done.3
  101.4 0.0 copy-start.4
  101.4 1.2 copy-done.4
  102.6 5.7 %attend.1 = (bf16[128,4096]{1,0:T(8,128)(2,1)}, bf16[128,1024]{1,0:T(8,128)(2,1)S(1)}) custom-call(bf16[128,4096]{1,0:T(8,128)(2,1)S(1)} %bitcast.12, bf16[128,4096]{1,0:T(8,128)(2,1)S(1)} %bitcast.13, bf16[128,1024]{1,0:T(8,128)(2,1)S(1)} %get-tuple-element.12.kv_ref, s32[128,1]{1,0:T(8,128)S(1)} %copy.9.col_ref, s32[1,128]{1,0:T(1,128)S(1)} %copy-done.5), custom_call_target="tpu_custom_call" | custom-call | tf_op jit(solution)/shard_map/attend/pallas_call | solution.py:251
  108.3 105.6 %post.1 = (bf16[128,8192]{1,0:T(8,128)(2,1)S(1)}, bf16[512,1024]{1,0:T(8,128)(2,1)S(1)}) custom-call(bf16[128,8192]{1,0:T(8,128)(2,1)S(1)} %get-tuple-element.10.x_ref, bf16[32,256,1024]{2,1,0:T(8,128)(2,1)} %get-tuple-element.11.whole_ref, bf16[128,1024]{1,0:T(8,128)(2,1)S(1)} %get-tuple-element.13.g_ref), custom_call_target="tpu_custom_call" | custom-call | tf_op jit(solution)/shard_map/post/pallas_call | solution.py:356
  214.0 0.0 copy-start.1
  214.0 1.3 copy-done.1
  215.3 3.0 %select_bitcast_fusion = bf16[1,128,8192]{2,1,0:T(8,128)(2,1)} fusion(bf16[128,8192]{1,0:T(8,128)(2,1)} %copy-done.1, pred[]{:T(512)S(6)} %eq.3), kind=kLoop, calls=%fused_computation | loop fusion | flops 1048576 | bytes 4194305 | tf_op jit(solution)/shard_map/broadcast_in_dim | solution.py:387
  218.4 1.0 copy.11
Async XLA Ops:
  0.6 100.7 %copy-start.5 = (s32[1,128]{1,0:T(1,128)S(1)}, s32[1,128]{1,0:T(1,128)}, u32[]{:S(2)}) copy-start(s32[1,128]{1,0:T(1,128)} %row_ref.1) | copy-start | bytes 1540
  0.6 1.6 copy-start
  2.2 1.2 copy-start.2
  3.5 0.7 copy-start.6
  4.1 97.3 %copy-start.3 = (bf16[1,128,4096]{2,1,0:T(8,128)(2,1)S(1)}, bf16[1,128,4096]{2,1,0:T(8,128)(2,1)}, u32[]{:S(2)}) copy-start(bf16[1,128,4096]{2,1,0:T(8,128)(2,1)} %param.7) | copy-start | bytes 3145732
  101.4 1.2 copy-start.4
  214.0 1.3 copy-start.1
